TPU v7x, 32 devices: a whole 2x2x4 slice. The times are simulated.
32 devices in a mesh: row: 4 (over y, x), col: 8 (over z, core).
Axes of the slice: x: 2, y: 2, z: 4, core: 2. Of those that a mesh axis runs over, the one named last changes fastest.
Arguments:
- matrix: float32 [4096, 4096], P('row', 'col'), may hold values from -8 to 48
- pivots: int32 [2, 128], replicated, may hold values from 256 to 4095, as said below
- lower_inverse: float32 [2, 128, 128], replicated, may hold values from -1 to 1, as said below
Outputs:
- factored: float32 [4096, 4096], P('row', 'col')
Inputs may be any that keep to these rules, and one draw needn't show every extreme that they name: pivots[k, j] is the global row that panel k exchanges with global row k * 128 + j; all 256 entries are distinct. Each lower_inverse[k] is unit lower triangular.
All inputs are finite; a program needn't handle non-finite values.
Results may differ from a plain program's by a relative error of at most 0.0001.
Values sent between devices are 32-bit elements; how exact they have to be, the bound alone decides.
A program may use at most 64 MiB of HBM per device.

v0:
```python
import jax
import jax.numpy as jnp
from jax import lax
from jax.sharding import PartitionSpec as P


def spread(value, axis, source):
    kept = jnp.where(lax.axis_index(axis) == source, value, 0).astype(value.dtype)
    return lax.psum(kept, axis)


def exact_dot(left, right):
    return jnp.dot(left, right, precision=lax.Precision.HIGHEST, preferred_element_type=jnp.float32)


def upper_inverse(upper):
    size = upper.shape[0]
    diag_vals = jnp.diagonal(upper)
    scaled = upper / diag_vals[:, None]
    eye_mat = jnp.eye(size, dtype=jnp.float32)
    power = eye_mat - scaled
    result = eye_mat + power
    reach = 2
    while reach < size:
        power = exact_dot(power, power)
        result = exact_dot(result, eye_mat + power)
        reach = reach * 2
    return result / diag_vals[None, :]


def on_device(matrix, pivots, lower_inverse):
    row_count = lax.axis_size("row")
    col_count = lax.axis_size("col")
    row_index = lax.axis_index("row")
    col_index = lax.axis_index("col")
    local_height, local_width = matrix.shape
    block_size = lower_inverse.shape[1]
    row_block = jnp.arange(local_height, dtype=jnp.int32) // block_size * row_count + row_index
    col_spots = jnp.arange(local_width, dtype=jnp.int32)
    col_block = col_spots // block_size * col_count + col_index
    col_inner = col_spots % block_size
    tri_rows = jnp.arange(block_size, dtype=jnp.int32)[:, None]
    height_spots = jnp.arange(local_height, dtype=jnp.int32)

    def owner_table(panel_num):
        pivot_rows = pivots[panel_num]
        pivot_block = pivot_rows // block_size
        is_owned = pivot_block % row_count == row_index
        local_rows = pivot_block // row_count * block_size + pivot_rows % block_size
        return (is_owned[:, None] & (local_rows[:, None] == height_spots[None, :])).astype(
            jnp.float32
        )

    factor_work = matrix
    for panel_num in range(pivots.shape[0]):
        pick_selector = owner_table(panel_num)
        pick_taken_rows = exact_dot(pick_selector, factor_work)
        pick_first_row = panel_num // row_count * block_size
        pick_is_root = panel_num % row_count == row_index
        pick_top_rows = jnp.where(
            pick_is_root, factor_work[pick_first_row : pick_first_row + block_size], 0.0
        )
        swap_taken_rows = pick_taken_rows
        swap_top_rows = pick_top_rows
        swap_taken_rows, swap_top_rows = lax.psum((swap_taken_rows, swap_top_rows), "row")
        place_factor_work = factor_work
        selector = owner_table(panel_num)
        hit_rows = jnp.sum(selector, axis=0) > 0.5
        placed = exact_dot(selector.T, swap_top_rows)
        place_factor_work = jnp.where(hit_rows[:, None], placed, place_factor_work)
        place_first_row = panel_num // row_count * block_size
        place_is_root = panel_num % row_count == row_index
        current = place_factor_work[place_first_row : place_first_row + block_size]
        factor_work = place_factor_work.at[place_first_row : place_first_row + block_size].set(
            jnp.where(place_is_root, swap_taken_rows, current)
        )
        full_factor_work = factor_work
        upper_factor_work = full_factor_work
        first_row = panel_num // row_count * block_size
        upper_block_rows = upper_factor_work[first_row : first_row + block_size]
        upper_is_root = panel_num % row_count == row_index
        product = exact_dot(lower_inverse[panel_num], upper_block_rows)
        diag_part = jnp.where(tri_rows <= col_inner[None, :], product, 0.0)
        upper_formed = spread(
            jnp.where(
                col_block[None, :] > panel_num,
                product,
                jnp.where(col_block[None, :] == panel_num, diag_part, upper_block_rows),
            ),
            "row",
            panel_num % row_count,
        )
        upper_factor_work = upper_factor_work.at[first_row : first_row + block_size].set(
            jnp.where(upper_is_root, upper_formed, upper_block_rows)
        )
        full_factor_work = upper_factor_work
        diag_first_col = panel_num // col_count * block_size
        lower_factor_work = full_factor_work
        lower_first_col = panel_num // col_count * block_size
        panel_cols = lower_factor_work[:, lower_first_col : lower_first_col + block_size]
        inverse_upper = upper_inverse(upper_formed[:, diag_first_col : diag_first_col + block_size])
        solved = exact_dot(panel_cols, inverse_upper)
        is_root = panel_num % col_count == col_index
        is_below = (row_block > panel_num)[:, None] & is_root
        lower_factor_work = lower_factor_work.at[
            :, lower_first_col : lower_first_col + block_size
        ].set(jnp.where(is_below, solved, panel_cols))
        lower_sent_panel = spread(jnp.where(is_below, solved, 0.0), "col", panel_num % col_count)
        full_factor_work = lower_factor_work
        change = exact_dot(lower_sent_panel, upper_formed)
        live = (row_block > panel_num)[:, None] & (col_block > panel_num)[None, :]
        factor_work = full_factor_work.at[:, 0 : 0 + local_width].set(
            jnp.where(live, full_factor_work - change, full_factor_work)
        )
    return factor_work


def solution(mesh):
    return jax.shard_map(
        on_device,
        mesh=mesh,
        in_specs=(P("row", "col"), P(), P()),
        out_specs=P("row", "col"),
        check_vma=False,
    )
```

profile of v0, /device:TPU:0, one launch (start us, length us, event | category | flops | bytes accessed | tf_op | source)
XLA Modules:
  0.0 351.4 jit_solution(4987288827838978806)
XLA Ops:
  6.5 0.9 fusion.56
  7.4 0.8 fusion.54
  8.2 1.7 slice_select_fusion.3
  9.9 3.2 fusion.7
  13.4 48.0 %all-reduce.19.cloned.1.call-done = (f32[128,512]{1,0:T(8,128)}, f32[128,512]{1,0:T(8,128)}) async-done(((f32[128,512]{1,0:T(8,128)}, f32[128,512]{1,0:T(8,128)}), (f32[128,512]{1,0:T(8,128)}, f32[128,512]{1,0:T(8,128)})) %all-reduce.19.cloned.1.call-update) | async-done | bytes 524304 | tf_op jit(solution)/shard_map/psum | solution.py:65
  61.4 2.1 convolution_select_fusion.1
  63.6 1.3 copy-done.3
  64.9 1.2 select_select_fusion.5
  66.1 0.7 compare_reduce_fusion
  66.8 1.6 copy.15
  68.4 40.7 %all-reduce.9.cloned.1.call-done = f32[128,512]{1,0:T(8,128)} async-done(((f32[128,512]{1,0:T(8,128)}), f32[128,512]{1,0:T(8,128)}) %all-reduce.9.cloned.1.call-update) | async-done | bytes 262160 | tf_op jit(solution)/shard_map/psum | solution.py:9
  109.2 0.9 slice.189
  110.1 1.2 gather_fusion
  111.3 1.2 fusion.47
  113.0 1.1 fusion.22
  114.1 0.2 fusion.23
  114.5 0.2 fusion.24
  114.9 0.2 fusion.25
  115.1 0.2 convolution_add_fusion.1
  115.3 0.2 fusion.26
  115.8 1.0 select_dynamic-update-slice_fusion.1
  116.8 0.6 fusion.12
  117.4 1.7 select_select_fusion.3
  119.2 56.2 %all-reduce.11.cloned.1.call-done = f32[1024,128]{1,0:T(8,128)} async-done(((f32[1024,128]{1,0:T(8,128)}), f32[1024,128]{1,0:T(8,128)}) %all-reduce.11.cloned.1.call-update) | async-done | bytes 524304 | tf_op jit(solution)/shard_map/psum | solution.py:9
  175.4 3.7 %subtract_select_fusion.1 = f32[1024,512]{1,0:T(8,128)S(1)} fusion(f32[1024,512]{1,0:T(8,128)} %copy-done, f32[1024,128]{1,0:T(8,128)} %all-reduce.11.cloned.1.call-done, f32[128,512]{1,0:T(8,128)S(1)} %copy-done.4, pred[512]{0:T(512)(128)(4,1)S(1)} %broadcast_compare_fusion.3, pred[1024]{0:T(1024)(128)(4,1)S(1)} %fusion.40), kind=kOutput, calls=%fused_computation.3 | convolution fusion | flops 806879232 | bytes 4982272 | tf_op jit(solution)/shard_map/dot_general | solution.py:13
  179.2 0.7 slice_select_fusion.1
  179.9 1.6 fusion.3
  181.8 44.3 %all-reduce.17.cloned.1.call-done = (f32[128,512]{1,0:T(8,128)}, f32[128,512]{1,0:T(8,128)}) async-done(((f32[128,512]{1,0:T(8,128)}, f32[128,512]{1,0:T(8,128)}), (f32[128,512]{1,0:T(8,128)}, f32[128,512]{1,0:T(8,128)})) %all-reduce.17.cloned.1.call-update) | async-done | bytes 524304 | tf_op jit(solution)/shard_map/psum | solution.py:65
  226.1 2.2 convolution_select_fusion
  228.3 1.3 copy-done.2
  229.6 1.2 select_select_fusion.4
  230.8 0.2 all-reduce.15.cloned.1.call-start
  231.1 1.6 copy.22
  232.7 41.2 %all-reduce.13.cloned.1.call-done = f32[128,512]{1,0:T(8,128)} async-done(((f32[128,512]{1,0:T(8,128)}), f32[128,512]{1,0:T(8,128)}) %all-reduce.13.cloned.1.call-update) | async-done | bytes 262160 | tf_op jit(solution)/shard_map/psum | solution.py:9
  273.9 0.9 slice.193
  274.8 1.2 gather_fusion.1
  276.1 1.2 fusion.48
  277.7 1.1 fusion.27
  278.8 0.2 fusion.28
  279.3 0.2 fusion.29
  279.7 0.2 fusion.30
  280.1 0.2 fusion.31
  280.3 0.2 convolution_divide_fusion
  280.5 1.0 select_dynamic-update-slice_fusion
  281.6 0.6 fusion.10
  282.1 1.7 select_select_fusion.2
  283.9 56.3 %all-reduce.15.cloned.1.call-done = f32[1024,128]{1,0:T(8,128)} async-done(((f32[1024,128]{1,0:T(8,128)}), f32[1024,128]{1,0:T(8,128)}) %all-reduce.15.cloned.1.call-update) | async-done | bytes 524304 | tf_op jit(solution)/shard_map/psum | solution.py:9
  340.2 4.4 %subtract_select_fusion = f32[1024,512]{1,0:T(8,128)} fusion(f32[1024,512]{1,0:T(8,128)S(1)} %get-tuple-element.126, f32[1024,128]{1,0:T(8,128)} %all-reduce.15.cloned.1.call-done, f32[128,512]{1,0:T(8,128)S(1)} %copy-done.5, pred[512]{0:T(512)(128)(4,1)S(1)} %broadcast_compare_fusion.5, pred[1024]{0:T(1024)(128)(4,1)S(1)} %fusion.41), kind=kOutput, calls=%fused_computation.2 | convolution fusion | flops 806879232 | bytes 4982272 | tf_op jit(solution)/shard_map/dot_general | solution.py:13
  (53 shorter events, 2.9 us)
Async XLA Ops:
  6.5 54.9 %copy-start.1 = (f32[1024,512]{1,0:T(8,128)S(1)}, f32[1024,512]{1,0:T(8,128)}, u32[]{:S(2)}) copy-start(f32[1024,512]{1,0:T(8,128)} %param.23) | copy-start | bytes 6291460
  6.5 54.9 %all-reduce.19.cloned.1.call-start = ((), (), s32[]{:S(2)}) async-start(), calls=%async_computation.5 | async-start | bytes 1048576 | tf_op jit(solution)/shard_map/psum | solution.py:65
  13.1 96.1 %all-reduce.9.cloned.1.call-start = ((), (), s32[]{:S(2)}) async-start(), calls=%async_computation | async-start | bytes 524288 | tf_op jit(solution)/shard_map/psum | solution.py:9
  61.4 3.5 copy-start.6
  61.4 3.5 copy-start.8
  63.6 1.3 copy-start.3
  66.1 109.3 %all-reduce.11.cloned.1.call-start = ((), (), s32[]{:S(2)}) async-start(), calls=%async_computation.1 | async-start | bytes 1048576 | tf_op jit(solution)/shard_map/psum | solution.py:9
  109.2 6.6 %copy-start.4 = (f32[128,512]{1,0:T(8,128)S(1)}, f32[128,512]{1,0:T(8,128)}, u32[]{:S(2)}) copy-start(f32[128,512]{1,0:T(8,128)} %all-reduce.9.cloned.1.call-done) | copy-start | bytes 786436
  119.1 56.3 %copy-start = (f32[1024,512]{1,0:T(8,128)}, f32[1024,512]{1,0:T(8,128)S(1)}, u32[]{:S(2)}) copy-start(f32[1024,512]{1,0:T(8,128)S(1)} %get-tuple-element.128) | copy-start | bytes 6291460
  119.1 107.0 %all-reduce.17.cloned.1.call-start = ((), (), s32[]{:S(2)}) async-start(), calls=%async_computation.4 | async-start | bytes 1048576 | tf_op jit(solution)/shard_map/psum | solution.py:65
  181.5 92.4 %all-reduce.13.cloned.1.call-start = ((), (), s32[]{:S(2)}) async-start(), calls=%async_computation.2 | async-start | bytes 524288 | tf_op jit(solution)/shard_map/psum | solution.py:9
  226.1 3.5 copy-start.7
  228.3 1.3 copy-start.2
  230.8 109.4 %all-reduce.15.cloned.1.call-start = ((), (), s32[]{:S(2)}) async-start(), calls=%async_computation.3 | async-start | bytes 1048576 | tf_op jit(solution)/shard_map/psum | solution.py:9
  273.9 6.6 %copy-start.5 = (f32[128,512]{1,0:T(8,128)S(1)}, f32[128,512]{1,0:T(8,128)}, u32[]{:S(2)}) copy-start(f32[128,512]{1,0:T(8,128)} %all-reduce.13.cloned.1.call-done) | copy-start | bytes 786436
Sparse Core Ops, SparseCore 0:
  13.2 48.1 all-reduce.18
  66.2 42.9 all-reduce.8
  119.3 56.1 all-reduce.10
  181.6 44.4 all-reduce.16
  230.9 42.9 all-reduce.12
  284.0 56.1 all-reduce.14
where the time goes:
time: 352 us; the launch traced here: 351 us
  waiting for transfers between devices  287 us (82%)
  matrix products  29.4 us (8%)
  between operations  13.9 us (4%)
  other arithmetic  10.7 us (3%)
  local copies, waits for them, and re-layouts  10.2 us (3%)
    psum x4, waiting for transfers between devices, spread(): return lax.psum(kept, axis)  194 us
    psum x2, waiting for transfers between devices, on_device(): lax.psum((swap_taken_rows, swap_top_rows), 'row')  92.4 us
    dot_general x34, matrix products, exact_dot(): jnp.dot(left, right, precision=lax.Precision.HIGHEST, preferred_element_t...  29.4 us
  transfers between devices with their start and end apart: 6, of which 6 were waited for; matrix products, arithmetic and copies ran while one was open for 1% of the time, Pallas kernels for 0%

commit v1 on v0

--- a/solution.py
+++ b/solution.py
@@ -6,7 +6,7 @@
 
 def spread(value, axis, source):
     kept = jnp.where(lax.axis_index(axis) == source, value, 0).astype(value.dtype)
-    return lax.psum(kept, axis)
+    return jnp.sum(lax.all_gather(kept, axis), axis=0)
 
 
 def exact_dot(left, right):

time: 352 us -> 302 us (0.86)
  waiting for transfers between devices: 287 us -> 236 us
  other arithmetic: 10.7 us -> 18.5 us
  matrix products: 29.4 us -> 24.6 us
    psum x4 -> x0, waiting for transfers between devices: 194 us -> none  [spread(): return lax.psum(kept, axis)]
    all_gather x0 -> x4, waiting for transfers between devices: none -> 144 us  [spread(): return jnp.sum(lax.all_gather(kept, axis), axis=0)]
    reduce_sum x0 -> x4, other arithmetic: none -> 7.58 us  [spread(): return jnp.sum(lax.all_gather(kept, axis), axis=0)]
    dot_general x34, matrix products: 29.4 us -> 24.6 us  [exact_dot(): jnp.dot(left, right, precision=lax.Precision.HIGHEST, preferred_element_t...]
where the time goes in v1:
time: 302 us
  waiting for transfers between devices  236 us (78%)
  matrix products  24.6 us (8%)
  other arithmetic  18.5 us (6%)
  between operations  13.9 us (5%)
  local copies, waits for them, and re-layouts  8.34 us (3%)
    all_gather x4, waiting for transfers between devices, spread(): return jnp.sum(lax.all_gather(kept, axis), axis=0)  144 us
    psum x2, waiting for transfers between devices, on_device(): lax.psum((swap_taken_rows, swap_top_rows), 'row')  92.2 us
    dot_general x34, matrix products, exact_dot(): jnp.dot(left, right, precision=lax.Precision.HIGHEST, preferred_element_t...  24.6 us
    reduce_sum x4, other arithmetic, spread(): return jnp.sum(lax.all_gather(kept, axis), axis=0)  7.58 us
  transfers between devices with their start and end apart: 6, of which 6 were waited for; matrix products, arithmetic and copies ran while one was open for 1% of the time, Pallas kernels for 0%

profile of v1, /device:TPU:0, one launch (start us, length us, event | category | flops | bytes accessed | tf_op | source)
XLA Modules:
  0.0 301.7 jit_solution(6749872421816810640)
XLA Ops:
  6.5 0.9 fusion.56
  7.4 0.8 fusion.54
  8.2 1.7 slice_select_fusion.3
  9.9 3.2 %fusion.7 = f32[128,512]{1,0:T(8,128)} fusion(f32[1024,512]{1,0:T(8,128)} %param.23, s32[128]{0:T(128)S(1)} %get-tuple-element.130, pred[128]{0:T(512)(128)(4,1)S(1)} %get-tuple-element.131), kind=kOutput, calls=%fused_computation.25 | convolution fusion | flops 805568512 | bytes 2359936 | tf_op jit(solution)/shard_map/dot_general | solution.py:13
  13.3 48.1 %all-reduce.7.cloned.1.call-done = (f32[128,512]{1,0:T(8,128)}, f32[128,512]{1,0:T(8,128)}) async-done(((f32[128,512]{1,0:T(8,128)}, f32[128,512]{1,0:T(8,128)}), (f32[128,512]{1,0:T(8,128)}, f32[128,512]{1,0:T(8,128)})) %all-reduce.7.cloned.1.call-update) | async-done | bytes 524304 | tf_op jit(solution)/shard_map/psum | solution.py:65
  61.4 2.1 convolution_select_fusion.1
  63.6 1.3 copy-done.3
  64.9 1.2 select_select_fusion.5
  66.1 0.7 compare_reduce_fusion
  66.8 1.6 copy.14
  68.5 24.3 %all-gather.9.cloned.1.call-done = f32[512,512]{1,0:T(8,128)} async-done(((f32[128,512]{1,0:T(8,128)}), f32[512,512]{1,0:T(8,128)}) %all-gather.9.cloned.1.call-update) | async-done | bytes 1048592 | tf_op jit(solution)/shard_map/all_gather | solution.py:9
  92.8 1.3 reduce_sum.56
  94.2 1.2 gather_fusion
  95.4 0.3 fusion.47
  95.7 0.3 fusion.22
  96.2 1.0 select_dynamic-update-slice_fusion.1
  97.4 0.2 fusion.23
  97.9 0.2 fusion.24
  98.3 0.2 fusion.25
  98.7 0.2 fusion.26
  99.1 0.6 fusion.12
  99.7 1.8 select_select_fusion.3
  101.6 47.2 %all-gather.11.cloned.1.call-done = f32[8192,128]{1,0:T(8,128)} async-done(((f32[1024,128]{1,0:T(8,128)}), f32[8192,128]{1,0:T(8,128)}) %all-gather.11.cloned.1.call-update) | async-done | bytes 4194320 | tf_op jit(solution)/shard_map/all_gather | solution.py:9
  148.8 2.5 reduce_sum.57
  151.3 3.6 %subtract_select_fusion.1 = f32[1024,512]{1,0:T(8,128)S(1)} fusion(f32[1024,512]{1,0:T(8,128)} %copy-done, f32[1024,128]{1,0:T(8,128)S(1)} %reduce_sum.57, f32[128,512]{1,0:T(8,128)S(1)} %reduce_sum.56, pred[512]{0:T(512)(128)(4,1)S(1)} %get-tuple-element.134, pred[1024]{0:T(1024)(128)(4,1)S(1)} %fusion.40), kind=kOutput, calls=%fused_computation.3 | convolution fusion | flops 806879232 | bytes 4982272 | tf_op jit(solution)/shard_map/dot_general | solution.py:13
  154.9 0.7 slice_select_fusion.1
  155.6 1.6 fusion.3
  157.5 44.1 %all-reduce.5.cloned.1.call-done = (f32[128,512]{1,0:T(8,128)}, f32[128,512]{1,0:T(8,128)}) async-done(((f32[128,512]{1,0:T(8,128)}, f32[128,512]{1,0:T(8,128)}), (f32[128,512]{1,0:T(8,128)}, f32[128,512]{1,0:T(8,128)})) %all-reduce.5.cloned.1.call-update) | async-done | bytes 524304 | tf_op jit(solution)/shard_map/psum | solution.py:65
  201.6 2.2 convolution_select_fusion
  203.8 1.3 copy-done.2
  205.1 1.2 select_select_fusion.4
  206.3 0.2 all-gather.15.cloned.1.call-start
  206.5 1.6 copy.19
  208.2 24.9 %all-gather.13.cloned.1.call-done = f32[512,512]{1,0:T(8,128)} async-done(((f32[128,512]{1,0:T(8,128)}), f32[512,512]{1,0:T(8,128)}) %all-gather.13.cloned.1.call-update) | async-done | bytes 1048592 | tf_op jit(solution)/shard_map/all_gather | solution.py:9
  233.1 1.3 reduce_sum.58
  234.4 1.2 gather_fusion.1
  235.7 0.3 fusion.48
  236.0 0.3 fusion.27
  236.4 1.0 select_dynamic-update-slice_fusion
  237.7 0.2 fusion.28
  238.1 0.2 fusion.29
  238.5 0.2 fusion.30
  239.0 0.2 fusion.31
  239.4 0.6 fusion.10
  240.0 1.8 select_select_fusion.2
  241.8 47.3 %all-gather.15.cloned.1.call-done = f32[8192,128]{1,0:T(8,128)} async-done(((f32[1024,128]{1,0:T(8,128)}), f32[8192,128]{1,0:T(8,128)}) %all-gather.15.cloned.1.call-update) | async-done | bytes 4194320 | tf_op jit(solution)/shard_map/all_gather | solution.py:9
  289.1 2.5 reduce_sum.59
  291.5 3.3 %subtract_select_fusion = f32[1024,512]{1,0:T(8,128)} fusion(f32[1024,512]{1,0:T(8,128)S(1)} %get-tuple-element.126, f32[1024,128]{1,0:T(8,128)S(1)} %reduce_sum.59, f32[128,512]{1,0:T(8,128)S(1)} %reduce_sum.58, pred[512]{0:T(512)(128)(4,1)S(1)} %broadcast_compare_fusion.5, pred[1024]{0:T(1024)(128)(4,1)S(1)} %fusion.41), kind=kOutput, calls=%fused_computation.2 | convolution fusion | flops 806879232 | bytes 4982272 | tf_op jit(solution)/shard_map/dot_general | solution.py:13
  (52 shorter events, 3.3 us)
Async XLA Ops:
  6.5 54.9 %copy-start.1 = (f32[1024,512]{1,0:T(8,128)S(1)}, f32[1024,512]{1,0:T(8,128)}, u32[]{:S(2)}) copy-start(f32[1024,512]{1,0:T(8,128)} %param.23) | copy-start | bytes 6291460
  6.5 54.9 %all-reduce.7.cloned.1.call-start = ((), (), s32[]{:S(2)}) async-start(), calls=%async_computation.5 | async-start | bytes 1048576 | tf_op jit(solution)/shard_map/psum | solution.py:65
  13.1 79.8 %all-gather.9.cloned.1.call-start = ((), (), s32[]{:S(2)}) async-start(), calls=%async_computation | async-start | bytes 1310720 | tf_op jit(solution)/shard_map/all_gather | solution.py:9
  61.4 3.5 %copy-start.4 = (f32[128,512]{1,0:T(8,128)S(1)}, f32[128,512]{1,0:T(8,128)}, u32[]{:S(2)}) copy-start(f32[128,512]{1,0:T(8,128)} %get-tuple-element.120) | copy-start | bytes 786436
  61.4 3.5 %copy-start.6 = (f32[2,128,128]{2,1,0:T(8,128)S(1)}, f32[2,128,128]{2,1,0:T(8,128)}, u32[]{:S(2)}) copy-start(f32[2,128,128]{2,1,0:T(8,128)} %param.25) | copy-start | bytes 393220
  63.5 1.3 copy-start.3
  66.1 82.8 %all-gather.11.cloned.1.call-start = ((), (), s32[]{:S(2)}) async-start(), calls=%async_computation.1 | async-start | bytes 4718592 | tf_op jit(solution)/shard_map/all_gather | solution.py:9
  101.5 49.8 %copy-start = (f32[1024,512]{1,0:T(8,128)}, f32[1024,512]{1,0:T(8,128)S(1)}, u32[]{:S(2)}) copy-start(f32[1024,512]{1,0:T(8,128)S(1)} %get-tuple-element.128) | copy-start | bytes 6291460
  101.5 100.1 %all-reduce.5.cloned.1.call-start = ((), (), s32[]{:S(2)}) async-start(), calls=%async_computation.4 | async-start | bytes 1048576 | tf_op jit(solution)/shard_map/psum | solution.py:65
  157.2 75.8 %all-gather.13.cloned.1.call-start = ((), (), s32[]{:S(2)}) async-start(), calls=%async_computation.2 | async-start | bytes 1310720 | tf_op jit(solution)/shard_map/all_gather | solution.py:9
  201.6 3.5 %copy-start.5 = (f32[128,512]{1,0:T(8,128)S(1)}, f32[128,512]{1,0:T(8,128)}, u32[]{:S(2)}) copy-start(f32[128,512]{1,0:T(8,128)} %get-tuple-element.118) | copy-start | bytes 786436
  203.8 1.3 copy-start.2
  206.3 82.8 %all-gather.15.cloned.1.call-start = ((), (), s32[]{:S(2)}) async-start(), calls=%async_computation.3 | async-start | bytes 4718592 | tf_op jit(solution)/shard_map/all_gather | solution.py:9
Sparse Core Ops, SparseCore 0:
  13.2 48.1 all-reduce.6
  66.2 26.6 all-gather.8
  101.7 47.1 all-gather.10
  157.4 44.1 all-reduce.4
  206.4 26.6 all-gather.12
  241.9 47.1 all-gather.14
